TPU v7x, 256 devices: a whole 4x4x8 slice. The times are simulated.
256 devices in a mesh: group: 2 (over y_lo), rows: 128 (over y_hi, z, x, core).
Axes of the slice: x: 4, y: 4 (y_hi: 2, y_lo: 2; y = y_hi * 2 + y_lo), z: 8, core: 2. Of those that a mesh axis runs over, the one named last changes fastest.
Arguments:
- embeds: bfloat16 [2, 16384, 768], P('group', 'rows'), may hold values from -8 to 8
- weights: bfloat16 [2, 768, 768], P('group', 'rows'), may hold values from -0.3 to 1.3
- pair_index: int32 [16384], replicated, may hold values from 0 to 16383, as said below
- scale: float32 [1], replicated, may hold values from 12 to 28
Outputs:
- embed_grad: bfloat16 [2, 16384, 768], P('group', 'rows')
- weight_grad: float32 [2, 768, 768], P('group', 'rows')
Inputs may be any that keep to these rules, and one draw needn't show every extreme that they name: `pair_index`: a permutation of the 16384 rows.
All inputs are finite; a program needn't handle non-finite values.
Results may differ from a plain program's by a relative error of at most 0.0062.
Values may be sent and summed in bfloat16 or wider, within the bound.
No kernel may reach another device: no remote copies, remote signals or barrier semaphores. Data moves between devices by JAX's collectives and lax.ppermute only.
A program may use at most 128 MiB of HBM per device.

v0:
```python
import jax
import jax.numpy as jnp
from jax import lax
from jax.sharding import PartitionSpec as P

EPS = 1e-06


def partner_2(block, axis, bit):
    count = lax.axis_size(axis)
    route = []
    for low in range(count):
        high = low | 1 << bit
        if high != low and high < count:
            route += [(low, high), (high, low)]
    return lax.ppermute(block, axis, route)


def per_device(embeds, weights, pair_index, scale):
    factor = scale[0]
    own_x = embeds[0]
    rows_here = own_x.shape[0]
    columns = own_x
    proj = jnp.dot(
        columns,
        lax.all_gather(weights[0], "rows", axis=0, tiled=True),
        preferred_element_type=jnp.float32,
    )
    inv = lax.rsqrt(jnp.sum(proj * proj, axis=1, keepdims=True) + EPS)
    unit = proj * inv
    low = unit.astype(jnp.bfloat16)
    block = partner_2(low, "group", 0)
    other = lax.all_gather(block, "rows", axis=0, tiled=True)
    total = other.shape[0]
    scores = factor * lax.dot_general(
        low, other, (((1,), (1,)), ((), ())), preferred_element_type=jnp.float32
    )
    own_lse = jnp.log(jnp.sum(jnp.exp(scores), axis=1))
    across = partner_2(own_lse, "group", 0)
    other_lse = lax.all_gather(across, "rows", axis=0, tiled=True)
    side = lax.axis_index("group")
    rank = lax.axis_index("rows")
    iota = jnp.arange(total, dtype=jnp.int32)
    inverse = jnp.zeros((total,), jnp.int32).at[pair_index].set(iota)
    table = jnp.where(side == 0, pair_index, inverse)
    partner = lax.dynamic_slice_in_dim(table, rank * rows_here, rows_here, 0)
    positive = jnp.take(other, partner, axis=0).astype(jnp.float32)
    weight_row = (jnp.exp(scores - own_lse[:, None]) + jnp.exp(scores - other_lse[None, :])).astype(
        jnp.bfloat16
    )
    d_unit = factor * (
        jnp.dot(weight_row, other, preferred_element_type=jnp.float32) - 2.0 * positive
    )
    d_proj = (inv * (d_unit - unit * jnp.sum(d_unit * unit, axis=1, keepdims=True))).astype(
        jnp.bfloat16
    )
    d_inputs = lax.dot_general(
        d_proj,
        lax.all_gather(weights[0], "rows", axis=0, tiled=True),
        (((1,), (1,)), ((), ())),
        preferred_element_type=jnp.float32,
    )
    columns = own_x
    d_weight = lax.psum_scatter(
        lax.dot_general(
            columns, d_proj, (((0,), (0,)), ((), ())), preferred_element_type=jnp.float32
        ),
        "rows",
        scatter_dimension=0,
        tiled=True,
    )
    return (d_inputs.astype(jnp.bfloat16)[None], d_weight[None])


def solution(mesh):
    return jax.shard_map(
        per_device,
        mesh=mesh,
        in_specs=(P("group", "rows", None), P("group", "rows", None), P(), P()),
        out_specs=(P("group", "rows", None), P("group", "rows", None)),
        check_vma=False,
    )
```

profile of v0, /device:TPU:2, one launch (start us, length us, event | category | flops | bytes accessed | tf_op | source)
XLA Modules:
  0.0 1761.5 jit_solution(17098865789082395145)
XLA Ops:
  7.2 0.0 copy-start
  7.2 0.0 all-gather.7.cloned.1.call-start
  7.2 1.4 copy.9
  8.6 0.0 all-gather.7.cloned.1.call-update
  8.6 0.0 all-gather.5.cloned.1.call-start
  8.7 122.2 %all-gather.7.cloned.1.call-done = bf16[1,768,768]{2,0,1:T(2,128)(2,1)} async-done(((bf16[1,6,768]{2,0,1:T(2,128)(2,1)}), bf16[1,768,768]{2,0,1:T(2,128)(2,1)}) %all-gather.7.cloned.1.call-update) | async-done | bytes 1179664 | tf_op jit(solution)/shard_map/all_gather | solution.py:26
  130.8 0.0 copy-done
  130.8 2.1 multiply_reduce_fusion.1
  132.9 0.1 multiply_convert_fusion.1
  133.0 0.7 collective-permute-start
  133.7 6.5 collective-permute-done
  140.2 0.0 copy-start.1
  140.2 0.7 copy-done.1
  140.9 0.0 all-gather.5.cloned.1.call-update
  140.9 0.0 all-reduce.3.cloned.1.call-start
  141.6 0.9 compare_select_fusion
  142.5 60.3 %scatter_custom_fusion = s32[16384]{0:T(1024)S(1)} fusion(s32[16384]{0:T(1024)S(1)} %compare_select_fusion, s32[16384]{0:T(1024)S(1)} %iota.3, s32[]{:T(128)} %constant.15.clone.1), kind=kCustom, calls=%fused_computation.27 | custom fusion | bytes 65540 | tf_op jit(solution)/shard_map/scatter | solution.py:44
  202.8 0.8 compare_and_fusion
  203.6 108.1 %all-gather.5.cloned.1.call-done = bf16[16384,768]{1,0:T(8,128)(2,1)} async-done(((bf16[128,768]{1,0:T(8,128)(2,1)}), bf16[16384,768]{1,0:T(8,128)(2,1)}) %all-gather.5.cloned.1.call-update) | async-done | bytes 25165840 | tf_op jit(solution)/shard_map/all_gather | solution.py:33
  311.7 14.8 exponential_reduce_fusion
  326.5 0.6 collective-permute-start.1
  327.1 12.4 gather_fusion
  339.5 0.0 collective-permute-done.1
  339.5 174.8 %all-gather.1 = f32[128,1,128]{2,1,0:T(1,128)S(1)} all-gather(f32[1,1,128]{2,1,0:T(1,128)S(1)} %bitcast.38), channel_id=1, replica_groups=mesh['group'=2,'rows'=128] {'rows'}, dimensions={0}, use_global_device_ids=true | all-gather | bytes 66048 | tf_op jit(solution)/shard_map/all_gather | solution.py:40
  514.3 0.0 copy-start.3
  514.3 0.0 copy-start.2
  514.3 14.0 multiply_reduce_fusion
  528.4 0.1 multiply_convert_fusion
  528.5 1.9 convolution_bitcast_fusion
  530.4 0.0 all-reduce.3.cloned.1.call-update
  530.4 0.0 copy-done.3
  530.5 0.6 dynamic-slice
  531.7 0.0 copy-done.2
  531.7 1.2 fusion.12
  532.9 1220.0 %all-reduce.3.cloned.1.call-done = f32[768,768]{0,1:T(8,128)} async-done(((f32[768,768]{0,1:T(8,128)}), f32[768,768]{0,1:T(8,128)}) %all-reduce.3.cloned.1.call-update) | async-done | bytes 2359312
  1752.9 1.3 dynamic-slice_bitcast_fusion
  1754.2 0.8 copy.10
  (4 shorter events, 0.0 us)
Async XLA Ops:
  7.2 123.7 %copy-start = (bf16[1,128,768]{2,1,0:T(8,128)(2,1)S(1)}, bf16[1,128,768]{2,1,0:T(8,128)(2,1)}, u32[]{:S(2)}) copy-start(bf16[1,128,768]{2,1,0:T(8,128)(2,1)} %param.4) | copy-start | bytes 589828
  7.2 123.7 %all-gather.7.cloned.1.call-start = ((), (), s32[]{:S(2)}) async-start(), calls=%async_computation.1 | async-start | bytes 2377728 | tf_op jit(solution)/shard_map/all_gather | solution.py:26
  8.6 303.1 %all-gather.5.cloned.1.call-start = ((), (), s32[]{:S(2)}) async-start(), calls=%async_computation | async-start | bytes 25362432 | tf_op jit(solution)/shard_map/all_gather | solution.py:33
  133.0 7.2 collective-permute-start
  140.2 0.7 copy-start.1
  140.9 1612.0 %all-reduce.3.cloned.1.call-start = ((), (), s32[]{:S(2)}) async-start(), calls=%async_computation.2 | async-start | bytes 4718592
  326.5 13.0 collective-permute-start.1
  514.3 16.1 copy-start.3
  514.3 17.4 copy-start.2
Sparse Core Ops, SparseCore 0:
  12.4 118.4 all-gather.6
  141.0 170.6 all-gather.4
  530.6 1222.3 all-reduce.2
where the time goes:
time: 1770 us; the launch traced here: 1760 us
  waiting for transfers between devices  1460 us (82%)
  blocking collectives  175 us (10%)
  local copies, waits for them, and re-layouts  77.4 us (4%)
  matrix products  34.1 us (2%)
    unnamed x4, waiting for transfers between devices  1220 us
    all_gather x1, blocking collectives, per_device(): other_lse = lax.all_gather(across, 'rows', axis=0, tiled=True)  175 us
    all_gather x1, waiting for transfers between devices, per_device(): lax.all_gather(weights[0], 'rows', axis=0, tiled=True)  122 us
    all_gather x1, waiting for transfers between devices, per_device(): other = lax.all_gather(block, 'rows', axis=0, tiled=True)  108 us
    scatter x1, local copies, waits for them, and re-layouts, per_device(): inverse = jnp.zeros((total,), jnp.int32).at[pair_index].set(iota)  60.3 us
  transfers between devices with their start and end apart: 5, of which 4 were waited for; matrix products, arithmetic and copies ran while one was open for 4% of the time, Pallas kernels for 0%

commit v1 on v0

v1 whole, which is shorter than its diff:
```python
import jax
import jax.numpy as jnp
from jax import lax
from jax.sharding import Mesh, PartitionSpec as P

EPS = 1e-06
AXES = ("yl", "yh", "z", "x", "c")
SIZES = {"yl": 2, "yh": 2, "z": 8, "x": 4, "c": 2}
ROWS = ("yh", "z", "x", "c")
PLANE = ("yl", "yh", "x")
F32 = jnp.float32
BF16 = jnp.bfloat16


def count(axes):
    total = 1
    for name in axes:
        total *= SIZES[name]
    return total


def mirror(value, axes, mask=1):
    return lax.ppermute(value, axes, [(i, i ^ mask) for i in range(count(axes))])


def gather(value, axes):
    copies = jnp.broadcast_to(value[None], (count(axes),) + value.shape)
    return lax.all_to_all(copies, axes, 0, 0)


def total(value, steps):
    for axes, mask in steps:
        value = value + mirror(value, axes, mask)
    return value


def gather_weights(shard):
    rows, width = shard.shape
    half = width // 2
    core = lax.axis_index("c")
    other = mirror(shard, ("c",))
    both = jnp.where(core == 0, jnp.stack([shard, other]), jnp.stack([other, shard]))
    both = both.reshape(2 * rows, width)
    part = lax.dynamic_slice_in_dim(both, core * half, half, 1)
    part = gather(part, ("yh", "x")).reshape(2, 4 * 2 * rows, half)
    part = gather(part, ("z",))
    part = jnp.swapaxes(part, 0, 1).reshape(width, half)
    other = mirror(part, ("c",))
    return jnp.where(
        core == 0,
        jnp.concatenate([part, other], 1),
        jnp.concatenate([other, part], 1),
    )


def scatter_weight_grad(partial):
    width = partial.shape[0]
    half = width // 2
    rows = width // 128
    core = lax.axis_index("c")
    mine = lax.dynamic_slice_in_dim(partial, core * half, half, 1)
    send = lax.dynamic_slice_in_dim(partial, (1 - core) * half, half, 1)
    part = mine + mirror(send, ("c",))
    part = part.astype(BF16).reshape(2, 8, 8 * rows, half)
    part = lax.all_to_all(jnp.swapaxes(part, 0, 1), ("z",), 0, 0)
    part = jnp.sum(part.astype(F32), axis=0).reshape(8, 2 * rows, half)
    part = jnp.sum(lax.all_to_all(part, ("yh", "x"), 0, 0), axis=0)
    part = part.reshape(2, rows, half)
    mine = lax.dynamic_index_in_dim(part, core, 0, False)
    other = mirror(lax.dynamic_index_in_dim(part, 1 - core, 0, False), ("c",))
    return jnp.where(
        core == 0,
        jnp.concatenate([mine, other], 1),
        jnp.concatenate([other, mine], 1),
    )


def per_device(embeds, weights, pair_index, scale):
    factor = scale[0]
    side = lax.axis_index("yl")
    yh, z, x, core = [lax.axis_index(name) for name in ROWS]
    own = embeds[0]
    here, width = own.shape
    half = here // 2
    weight = gather_weights(weights[0])
    proj = jnp.dot(own, weight, preferred_element_type=F32)
    inv = lax.rsqrt(jnp.sum(proj * proj, axis=1, keepdims=True) + EPS)
    unit = proj * inv
    low = unit.astype(BF16)

    keep = lax.dynamic_slice_in_dim(low, side * half, half, 0)
    send = lax.dynamic_slice_in_dim(low, (1 - side) * half, half, 0)
    came = mirror(send, ("yl",))
    image = jnp.where(side == 0, keep, came)
    modal = jnp.where(side == 0, came, keep)

    image = gather(image, PLANE).reshape(16 * half, width)
    modal = gather(modal, ("z",)).reshape(8 * half, width)
    other = mirror(modal, ("c",))
    modal = jnp.where(
        core == 0, jnp.concatenate([modal, other]), jnp.concatenate([other, modal])
    )

    table = pair_index.reshape(2, 8, 4, 2, 2, half)
    table = lax.dynamic_index_in_dim(table, z, 1, False)
    table = lax.dynamic_index_in_dim(table, core, 2, False)
    partner = table.transpose(2, 0, 1, 3).reshape(16 * half)
    cc, zz, rr = jnp.arange(2), jnp.arange(8), jnp.arange(half)
    ids = (((yh * 8 + zz[None, :, None]) * 4 + x) * 2 + cc[:, None, None]) * here
    ids = (ids + side * half + rr[None, None, :]).reshape(16 * half)

    scores = factor * lax.dot_general(
        image, modal, (((1,), (1,)), ((), ())), preferred_element_type=F32
    )
    power = jnp.exp(scores)
    row_sum = total(
        jnp.sum(power, axis=1), [(("x",), 1), (("x",), 3), (("yl", "yh"), 2), (("yl", "yh"), 3)]
    )
    col_sum = total(
        jnp.sum(power, axis=0), [(("c",), 1), (("z",), 1), (("z",), 2), (("z",), 4)]
    )
    hit = partner[:, None] == ids[None, :]
    weight_row = power * (1.0 / row_sum[:, None] + 1.0 / col_sum[None, :])
    weight_row = (weight_row - jnp.where(hit, 2.0, 0.0)).astype(BF16)

    d_modal = lax.dot_general(
        weight_row, image, (((0,), (0,)), ((), ())), preferred_element_type=F32
    )
    d_modal = d_modal.reshape(2, 8 * half, width)
    mine = lax.dynamic_index_in_dim(d_modal, core, 0, False)
    send = lax.dynamic_index_in_dim(d_modal, 1 - core, 0, False).astype(BF16)
    d_modal = (mine + mirror(send, ("c",)).astype(F32)).astype(BF16)
    d_modal = lax.all_to_all(d_modal.reshape(8, half, width), ("z",), 0, 0)
    d_modal = jnp.sum(d_modal.astype(F32), axis=0)

    d_image = jnp.dot(weight_row, modal, preferred_element_type=F32).astype(BF16)
    d_image = lax.all_to_all(d_image.reshape(16, half, width), PLANE, 0, 0)
    d_image = jnp.sum(d_image.astype(F32), axis=0)

    came = mirror(jnp.where(side == 0, d_modal, d_image), ("yl",))
    d_unit = jnp.where(
        side == 0,
        jnp.concatenate([d_image, came]),
        jnp.concatenate([came, d_modal]),
    )
    d_unit = factor * d_unit
    d_proj = inv * (d_unit - unit * jnp.sum(d_unit * unit, axis=1, keepdims=True))
    d_proj = d_proj.astype(BF16)
    d_inputs = lax.dot_general(
        d_proj, weight, (((1,), (1,)), ((), ())), preferred_element_type=F32
    )
    d_weight = lax.dot_general(
        own, d_proj, (((0,), (0,)), ((), ())), preferred_element_type=F32
    )
    return (d_inputs.astype(BF16)[None], scatter_weight_grad(d_weight)[None])


def solution(mesh):
    devices = mesh.devices.reshape([SIZES[name] for name in AXES])
    return jax.shard_map(
        per_device,
        mesh=Mesh(devices, AXES),
        in_specs=(P("yl", ROWS, None), P("yl", ROWS, None), P(), P()),
        out_specs=(P("yl", ROWS, None), P("yl", ROWS, None)),
        check_vma=False,
    )
```

time: 1770 us -> 238 us (0.13)
  waiting for transfers between devices: 1460 us -> 79.7 us
  blocking collectives: 175 us -> 99.8 us
  local copies, waits for them, and re-layouts: 77.4 us -> 8.47 us
  starting transfers between devices: 1.38 us -> 21.5 us
    unnamed x4 -> x0, waiting for transfers between devices: 1220 us -> none
    all_gather x2 -> x0, waiting for transfers between devices: 230 us -> none  [the longest x1 122 us: per_device(): lax.all_gather(weights[0], 'rows', axis=0, tiled=True)]
    all_gather x1 -> x0, blocking collectives: 175 us -> none  [per_device(): other_lse = lax.all_gather(across, 'rows', axis=0, tiled=True)]
    all_to_all x0 -> x5, blocking collectives: none -> 99.8 us  [the longest x3 65.3 us: gather(): return lax.all_to_all(copies, axes, 0, 0)]
    scatter x1 -> x0, local copies, waits for them, and re-layouts: 60.3 us -> none  [per_device(): inverse = jnp.zeros((total,), jnp.int32).at[pair_index].set(iota)]
    all_to_all x0 -> x3, waiting for transfers between devices: none -> 50.9 us  [the longest x1 19.7 us: gather(): return lax.all_to_all(copies, axes, 0, 0)]
    ppermute x2 -> x16, waiting for transfers between devices: 6.49 us -> 28.9 us  [mirror(): lax.ppermute(value, axes, [(i, i ^ mask) for i in range(count(axes))])]
  transfers between devices with their start and end apart: 5 -> 19, of which waited for: 4 -> 14; matrix products, arithmetic and copies ran while one was open for 4% -> 5% of each run, Pallas kernels for 0% -> 0%
where the time goes in v1:
time: 238 us; the launch traced here: 235 us
  blocking collectives  99.8 us (42%)
  waiting for transfers between devices  79.7 us (33%)
  starting transfers between devices  21.5 us (9%)
  matrix products  16.8 us (7%)
  local copies, waits for them, and re-layouts  8.47 us (4%)
  other arithmetic  6.85 us (3%)
    all_to_all x3, blocking collectives, gather(): return lax.all_to_all(copies, axes, 0, 0)  65.3 us
    ppermute x16, waiting for transfers between devices, mirror(): lax.ppermute(value, axes, [(i, i ^ mask) for i in range(count(axes))])  28.9 us
    all_to_all x1, blocking collectives, scatter_weight_grad(): part = lax.all_to_all(jnp.swapaxes(part, 0, 1), ('z',), 0, 0)  22 us
    all_to_all x1, waiting for transfers between devices, gather(): return lax.all_to_all(copies, axes, 0, 0)  19.7 us
    all_to_all x1, waiting for transfers between devices, per_device(): d_modal = lax.all_to_all(d_modal.reshape(8, half, width), ('z',), 0, 0)  18.6 us
    all_to_all x1, waiting for transfers between devices, per_device(): d_image = lax.all_to_all(d_image.reshape(16, half, width), PLANE, 0, 0)  12.5 us
    all_to_all x1, blocking collectives, scatter_weight_grad(): part = jnp.sum(lax.all_to_all(part, ('yh', 'x'), 0, 0), axis=0)  12.4 us
    ppermute x16, starting transfers between devices, mirror(): lax.ppermute(value, axes, [(i, i ^ mask) for i in range(count(axes))])  7.6 us
  transfers between devices with their start and end apart: 19, of which 14 were waited for; matrix products, arithmetic and copies ran while one was open for 5% of the time, Pallas kernels for 0%

profile of v1, /device:TPU:2, one launch (start us, length us, event | category | flops | bytes accessed | tf_op | source)
XLA Modules:
  0.0 234.8 jit_solution(15794371563804418394)
XLA Ops:
  0.8 1.4 collective-permute-done
  2.1 0.8 maximum_select_fusion.7
  3.0 14.0 %all_to_all.40 = bf16[8,12,384]{2,1,0:T(8,128)(2,1)S(1)} all-to-all(bf16[8,12,384]{2,1,0:T(8,128)(2,1)S(1)} %broadcast_in_dim.18), channel_id=1, replica_groups=mesh['yl'=2,'yh'=2,'z'=8,'x'=4,'c'=2] {'yh','x'}, dimensions={0} | all-to-all | bytes 147456 | tf_op jit(solution)/shard_map/all_to_all | solution.py:28
  17.1 26.1 %all_to_all.41 = bf16[8,2,48,384]{3,2,1,0:T(8,128)(2,1)S(1)} all-to-all(bf16[8,2,48,384]{3,2,1,0:T(8,128)(2,1)S(1)} %broadcast_in_dim.20), channel_id=1, replica_groups=mesh['yl'=2,'yh'=2,'z'=8,'x'=4,'c'=2] {'z'}, dimensions={0} | all-to-all | bytes 1179648 | tf_op jit(solution)/shard_map/all_to_all | solution.py:28
  43.3 2.0 collective-permute-done.1
  45.3 0.6 multiply_reduce_fusion
  45.9 0.3 copy-done.6
  46.3 0.8 collective-permute-start.2
  47.1 4.2 %collective-permute-done.2 = bf16[64,768]{1,0:T(8,128)(2,1)S(1)} collective-permute-done((bf16[64,768]{1,0:T(8,128)(2,1)S(1)}, bf16[64,768]{1,0:T(8,128)(2,1)S(1)}, u32[]{:S(2)}, u32[]{:S(2)}) %collective-permute-start.2) | collective-permute-done | bytes 98336 | tf_op jit(solution)/shard_map/ppermute | solution.py:23
  51.3 25.3 %all_to_all.42 = bf16[8,64,768]{2,1,0:T(8,128)(2,1)S(1)} all-to-all(bf16[8,64,768]{2,1,0:T(8,128)(2,1)S(1)} %broadcast_in_dim.22), channel_id=1, replica_groups=mesh['yl'=2,'yh'=2,'z'=8,'x'=4,'c'=2] {'z'}, dimensions={0} | all-to-all | bytes 1572864 | tf_op jit(solution)/shard_map/all_to_all | solution.py:28
  76.6 1.3 broadcast_in_dim.21
  77.9 4.7 %all-to-all-start.2 = ((bf16[16,64,768]{2,1,0:T(8,128)(2,1)}), bf16[16,64,768]{2,1,0:T(8,128)(2,1)S(1)}, u32[]{:S(2)}, u32[]{:S(2)}) async-start(bf16[16,64,768]{2,1,0:T(8,128)(2,1)} %broadcast_in_dim.21), calls=%async_computation.2 | async-start | bytes 3145728 | tf_op jit(solution)/shard_map/all_to_all | solution.py:28
  83.3 19.7 %all-to-all-done.2 = bf16[16,64,768]{2,1,0:T(8,128)(2,1)S(1)} async-done(((bf16[16,64,768]{2,1,0:T(8,128)(2,1)}), bf16[16,64,768]{2,1,0:T(8,128)(2,1)S(1)}, u32[]{:S(2)}, u32[]{:S(2)}) %all-to-all-start.2) | async-done | bytes 1572896 | tf_op jit(solution)/shard_map/all_to_all | solution.py:28
  103.0 5.9 %fusion.29 = (f32[1024]{0:T(1024)S(1)}, f32[1024]{0:T(1024)S(1)}, f32[1024,1024]{0,1:T(8,128)}) fusion(bf16[1024,768]{1,0:T(8,128)(2,1)S(1)} %bitcast.75, bf16[512,768]{1,0:T(8,128)(2,1)} %collective-permute-done.3, bf16[512,768]{1,0:T(8,128)(2,1)S(1)} %bitcast.79, pred[]{:T(512)S(6)} %eq.34, f32[]{:T(128)} %bitcast.69), kind=kOutput, calls=%fused_computation.64 | convolution fusion | flops 1620834304 | bytes 7348229 | tf_op jit(solution)/shard_map/dot_general | solution.py:112
  108.9 1.7 collective-permute-start.4
  110.7 0.5 collective-permute-start.9
  111.1 1.5 collective-permute-done.4
  112.6 0.2 collective-permute-start.5
  112.8 1.4 collective-permute-done.9
  114.4 0.1 reshape.163
  114.5 1.7 collective-permute-done.5
  116.2 0.2 collective-permute-start.6
  116.5 2.3 collective-permute-done.10
  118.8 2.2 collective-permute-start.11
  121.1 5.4 %copy.19 = f32[1024,1024]{1,0:T(8,128)} copy(f32[1024,1024]{0,1:T(8,128)} %get-tuple-element.20) | data formatting | bytes 8388608 | tf_op jit(solution)/shard_map/exp | solution.py:115
  126.5 1.0 collective-permute-start.7
  127.6 4.0 %collective-permute-done.7 = f32[1024]{0:T(1024)S(1)} collective-permute-done((f32[1024]{0:T(1024)S(1)}, f32[1024]{0:T(1024)S(1)}, u32[]{:S(2)}, u32[]{:S(2)}) %collective-permute-start.7) | collective-permute-done | bytes 4128 | tf_op jit(solution)/shard_map/ppermute | solution.py:23
  131.6 3.8 %fusion.1 = bf16[1024,1024]{1,0:T(8,128)(2,1)} fusion(f32[1024,1024]{0,1:T(8,128)} %get-tuple-element.20, s32[1024]{0:T(1024)S(1)} %eq.36, f32[1024]{0:T(1024)S(1)} %add_divide_fusion, f32[1024]{0:T(1024)S(1)} %add_divide_fusion.1, s32[1024]{0:T(1024)S(1)} %add.198), kind=kLoop, calls=%fused_computation.2 | loop fusion | flops 6291456 | bytes 6307840 | tf_op jit(solution)/shard_map/convert_element_type | solution.py:124
  135.5 4.7 %fusion.9 = bf16[1024,768]{1,0:T(8,128)(2,1)} fusion(f32[1024,1024]{1,0:T(8,128)S(1)} %copy-done.1, s32[1024]{0:T(1024)S(1)} %add.198, f32[1024]{0:T(1024)S(1)} %add_divide_fusion, f32[1024]{0:T(1024)S(1)} %add_divide_fusion.1, s32[1024]{0:T(1024)S(1)} %eq.36, bf16[512,768]{1,0:T(8,128)(2,1)} %collective-permute-done.3, bf16[512,768]{1,0:T(8,128)(2,1)S(1)} %bitcast.80, ...), kind=kOutput, calls=%fused_computation.13 | convolution fusion | flops 1624768512 | bytes 7356417 | tf_op jit(solution)/shard_map/dot_general | solution.py:136
  140.2 4.7 %all-to-all-start.4 = ((bf16[16,64,768]{2,1,0:T(8,128)(2,1)}), bf16[16,64,768]{2,1,0:T(8,128)(2,1)S(1)}, u32[]{:S(2)}, u32[]{:S(2)}) async-start(bf16[16,64,768]{2,1,0:T(8,128)(2,1)} %bitcast.77), calls=%async_computation.4 | async-start | bytes 3145728 | tf_op jit(solution)/shard_map/all_to_all | solution.py:137
  144.9 3.8 %fusion.30 = f32[2,512,768]{2,1,0:T(8,128)S(1)} fusion(bf16[2,512,1024]{2,1,0:T(8,128)(2,1)} %bitcast.74, bf16[1024,768,1]{1,0,2:T(8,128)(2,1)} %bitcast.76), kind=kOutput, calls=%fused_computation.65 | convolution fusion | flops 1610612736 | bytes 6815744 | tf_op jit(solution)/shard_map/dot_general | solution.py:126
  149.0 2.3 collective-permute-done.12
  151.2 1.0 fusion.10
  152.3 12.5 %all-to-all-done.4 = bf16[16,64,768]{2,1,0:T(8,128)(2,1)S(1)} async-done(((bf16[16,64,768]{2,1,0:T(8,128)(2,1)}), bf16[16,64,768]{2,1,0:T(8,128)(2,1)S(1)}, u32[]{:S(2)}, u32[]{:S(2)}) %all-to-all-start.4) | async-done | bytes 1572896 | tf_op jit(solution)/shard_map/all_to_all | solution.py:137
  164.8 4.5 %all-to-all-start.5 = ((bf16[8,64,768]{2,1,0:T(8,128)(2,1)}), bf16[8,64,768]{2,1,0:T(8,128)(2,1)S(1)}, u32[]{:S(2)}, u32[]{:S(2)}) async-start(bf16[8,64,768]{2,1,0:T(8,128)(2,1)} %bitcast.71), calls=%async_computation.5 | async-start | bytes 1572864 | tf_op jit(solution)/shard_map/all_to_all | solution.py:133
  169.3 0.2 convert_reduce_fusion
  169.6 18.6 %all-to-all-done.5 = bf16[8,64,768]{2,1,0:T(8,128)(2,1)S(1)} async-done(((bf16[8,64,768]{2,1,0:T(8,128)(2,1)}), bf16[8,64,768]{2,1,0:T(8,128)(2,1)S(1)}, u32[]{:S(2)}, u32[]{:S(2)}) %all-to-all-start.5) | async-done | bytes 786464 | tf_op jit(solution)/shard_map/all_to_all | solution.py:133
  188.3 0.4 collective-permute-start.13
  188.7 5.3 %collective-permute-done.13 = f32[64,768]{1,0:T(8,128)S(1)} collective-permute-done((f32[64,768]{1,0:T(8,128)S(1)}, f32[64,768]{1,0:T(8,128)S(1)}, u32[]{:S(2)}, u32[]{:S(2)}) %collective-permute-start.13) | collective-permute-done | bytes 196640 | tf_op jit(solution)/shard_map/ppermute | solution.py:23
  194.1 0.2 fusion.15
  194.3 0.2 fusion.18
  194.5 0.5 fusion.20
  195.2 2.8 %collective-permute-done.14 = f32[768,384]{1,0:T(8,128)S(1)} collective-permute-done((f32[768,384]{1,0:T(8,128)S(1)}, f32[768,384]{1,0:T(8,128)S(1)}, u32[]{:S(2)}, u32[]{:S(2)}) %collective-permute-start.14) | collective-permute-done | bytes 1179680 | tf_op jit(solution)/shard_map/ppermute | solution.py:23
  198.0 0.1 fusion.11
  198.2 22.0 %all_to_all.43 = bf16[8,2,48,384]{3,2,1,0:T(8,128)(2,1)S(1)} all-to-all(bf16[8,2,48,384]{3,2,1,0:T(8,128)(2,1)S(1)} %bitcast.72), channel_id=1, replica_groups=mesh['yl'=2,'yh'=2,'z'=8,'x'=4,'c'=2] {'z'}, dimensions={0} | all-to-all | bytes 1179648 | tf_op jit(solution)/shard_map/all_to_all | solution.py:65
  220.3 12.4 %all_to_all.44 = f32[8,12,384]{2,1,0:T(8,128)S(1)} all-to-all(f32[8,12,384]{2,1,0:T(8,128)S(1)} %reshape.167), channel_id=1, replica_groups=mesh['yl'=2,'yh'=2,'z'=8,'x'=4,'c'=2] {'yh','x'}, dimensions={0} | all-to-all | bytes 294912 | tf_op jit(solution)/shard_map/all_to_all | solution.py:67
  232.9 1.2 fusion.12
  234.2 0.6 copy.22
  (65 shorter events, 1.7 us)
Async XLA Ops:
  0.6 44.7 %copy-start = (bf16[1,128,768]{2,1,0:T(8,128)(2,1)S(1)}, bf16[1,128,768]{2,1,0:T(8,128)(2,1)}, u32[]{:S(2)}) copy-start(bf16[1,128,768]{2,1,0:T(8,128)(2,1)} %param.4) | copy-start | bytes 589828
  0.6 1.5 collective-permute-start
  43.2 2.7 %copy-start.3 = (bf16[8,2,48,384]{3,2,0,1:T(8,128)(2,1)}, bf16[8,2,48,384]{3,2,0,1:T(8,128)(2,1)S(1)}, u32[]{:S(2)}) copy-start(bf16[8,2,48,384]{3,2,0,1:T(8,128)(2,1)S(1)} %copy.18) | copy-start | bytes 1769476
  43.2 2.1 collective-permute-start.1
  45.3 0.9 copy-start.6
  46.3 4.9 %collective-permute-start.2 = (bf16[64,768]{1,0:T(8,128)(2,1)S(1)}, bf16[64,768]{1,0:T(8,128)(2,1)S(1)}, u32[]{:S(2)}, u32[]{:S(2)}) collective-permute-start(bf16[64,768]{1,0:T(8,128)(2,1)S(1)} %constant_dynamic-slice_fusion.1), channel_id=1, source_target_pairs={{0,128},{128,0},{1,129},{129,1},{2,130},{130,2},{3,131},{131,3},{4... | collective-permute-start | bytes 294920 | tf_op jit(solution)/shard_map/ppermute | solution.py:23
  77.9 25.1 %all-to-all-start.2 = ((bf16[16,64,768]{2,1,0:T(8,128)(2,1)}), bf16[16,64,768]{2,1,0:T(8,128)(2,1)S(1)}, u32[]{:S(2)}, u32[]{:S(2)}) async-start(bf16[16,64,768]{2,1,0:T(8,128)(2,1)} %broadcast_in_dim.21), calls=%async_computation.2 | async-start | bytes 3145728 | tf_op jit(solution)/shard_map/all_to_all | solution.py:28
  82.6 20.4 %collective-permute-start.3 = (bf16[512,768]{1,0:T(8,128)(2,1)S(1)}, bf16[512,768]{1,0:T(8,128)(2,1)}, u32[]{:S(2)}, u32[]{:S(2)}) collective-permute-start(bf16[512,768]{1,0:T(8,128)(2,1)S(1)} %bitcast.78), channel_id=1, source_target_pairs={{0,1},{1,0},{2,3},{3,2},{4,5},{5,4},{6,7},{7,6},{8,9},{9,8},{10,11... | collective-permute-start | bytes 2359304 | tf_op jit(solution)/shard_map/ppermute | solution.py:23
  103.0 5.9 %copy-start.2 = (bf16[16,64,768]{2,1,0:T(8,128)(2,1)}, bf16[16,64,768]{2,1,0:T(8,128)(2,1)S(1)}, u32[]{:S(2)}) copy-start(bf16[16,64,768]{2,1,0:T(8,128)(2,1)S(1)} %all-to-all-done.2) | copy-start | bytes 4718596
  103.0 11.4 %copy-start.5 = (s32[16384]{0:T(1024)S(1)}, s32[16384]{0:T(1024)}, u32[]{:S(2)}) copy-start(s32[16384]{0:T(1024)} %param.6) | copy-start | bytes 196612
  108.9 1.7 collective-permute-start.8
  108.9 3.7 %collective-permute-start.4 = (f32[1024]{0:T(1024)S(1)}, f32[1024]{0:T(1024)S(1)}, u32[]{:S(2)}, u32[]{:S(2)}) collective-permute-start(f32[1024]{0:T(1024)S(1)} %get-tuple-element.12), channel_id=1, source_target_pairs={{0,2},{2,0},{4,6},{6,4},{1,3},{3,1},{5,7},{7,5},{8,10},{10,8},{12,... | collective-permute-start | bytes 12296 | tf_op jit(solution)/shard_map/ppermute | solution.py:23
  110.7 3.6 %collective-permute-start.9 = (f32[1024]{0:T(1024)S(1)}, f32[1024]{0:T(1024)S(1)}, u32[]{:S(2)}, u32[]{:S(2)}) collective-permute-start(f32[1024]{0:T(1024)S(1)} %add.178), channel_id=1, source_target_pairs={{0,8},{8,0},{16,24},{24,16},{32,40},{40,32},{48,56},{56,48},{1,9},... | collective-permute-start | bytes 12296 | tf_op jit(solution)/shard_map/ppermute | solution.py:23
  112.6 3.6 %collective-permute-start.5 = (f32[1024]{0:T(1024)S(1)}, f32[1024]{0:T(1024)S(1)}, u32[]{:S(2)}, u32[]{:S(2)}) collective-permute-start(f32[1024]{0:T(1024)S(1)} %add.173), channel_id=1, source_target_pairs={{0,6},{2,4},{4,2},{6,0},{1,7},{3,5},{5,3},{7,1},{8,14},{10,12},{12... | collective-permute-start | bytes 12296 | tf_op jit(solution)/shard_map/ppermute | solution.py:23
  114.3 4.5 %collective-permute-start.10 = (f32[1024]{0:T(1024)S(1)}, f32[1024]{0:T(1024)S(1)}, u32[]{:S(2)}, u32[]{:S(2)}) collective-permute-start(f32[1024]{0:T(1024)S(1)} %add.179), channel_id=1, source_target_pairs={{0,16},{8,24},{16,0},{24,8},{32,48},{40,56},{48,32},{56,40},{1,17}... | collective-permute-start | bytes 12296 | tf_op jit(solution)/shard_map/ppermute | solution.py:23
  116.2 10.3 %collective-permute-start.6 = (f32[1024]{0:T(1024)S(1)}, f32[1024]{0:T(1024)S(1)}, u32[]{:S(2)}, u32[]{:S(2)}) collective-permute-start(f32[1024]{0:T(1024)S(1)} %add.174), channel_id=1, source_target_pairs={{0,128},{64,192},{128,0},{192,64},{1,129},{65,193},{129,1},{193,65... | collective-permute-start | bytes 12296 | tf_op jit(solution)/shard_map/ppermute | solution.py:23
  118.8 8.8 %collective-permute-start.11 = (f32[1024]{0:T(1024)S(1)}, f32[1024]{0:T(1024)S(1)}, u32[]{:S(2)}, u32[]{:S(2)}) collective-permute-start(f32[1024]{0:T(1024)S(1)} %add.180), channel_id=1, source_target_pairs={{0,32},{8,40},{16,48},{24,56},{32,0},{40,8},{48,16},{56,24},{1,33}... | collective-permute-start | bytes 12296 | tf_op jit(solution)/shard_map/ppermute | solution.py:23
  126.5 5.1 %collective-permute-start.7 = (f32[1024]{0:T(1024)S(1)}, f32[1024]{0:T(1024)S(1)}, u32[]{:S(2)}, u32[]{:S(2)}) collective-permute-start(f32[1024]{0:T(1024)S(1)} %add.175), channel_id=1, source_target_pairs={{0,192},{64,128},{128,64},{192,0},{1,193},{65,129},{129,65},{193,1... | collective-permute-start | bytes 12296 | tf_op jit(solution)/shard_map/ppermute | solution.py:23
  131.6 3.9 %copy-start.1 = (f32[1024,1024]{1,0:T(8,128)S(1)}, f32[1024,1024]{1,0:T(8,128)}, u32[]{:S(2)}) copy-start(f32[1024,1024]{1,0:T(8,128)} %copy.19) | copy-start | bytes 12582916
  140.2 24.6 %all-to-all-start.4 = ((bf16[16,64,768]{2,1,0:T(8,128)(2,1)}), bf16[16,64,768]{2,1,0:T(8,128)(2,1)S(1)}, u32[]{:S(2)}, u32[]{:S(2)}) async-start(bf16[16,64,768]{2,1,0:T(8,128)(2,1)} %bitcast.77), calls=%async_computation.4 | async-start | bytes 3145728 | tf_op jit(solution)/shard_map/all_to_all | solution.py:137
  148.9 2.4 %collective-permute-start.12 = (bf16[512,768]{1,0:T(8,128)(2,1)S(1)}, bf16[512,768]{1,0:T(8,128)(2,1)S(1)}, u32[]{:S(2)}, u32[]{:S(2)}) collective-permute-start(bf16[512,768]{1,0:T(8,128)(2,1)S(1)} %fusion.13), channel_id=1, source_target_pairs={{0,1},{1,0},{2,3},{3,2},{4,5},{5,4},{6,7},{7,6},{8,9},{9,8},{10,11... | collective-permute-start | bytes 2359304 | tf_op jit(solution)/shard_map/ppermute | solution.py:23
  164.8 23.3 %all-to-all-start.5 = ((bf16[8,64,768]{2,1,0:T(8,128)(2,1)}), bf16[8,64,768]{2,1,0:T(8,128)(2,1)S(1)}, u32[]{:S(2)}, u32[]{:S(2)}) async-start(bf16[8,64,768]{2,1,0:T(8,128)(2,1)} %bitcast.71), calls=%async_computation.5 | async-start | bytes 1572864 | tf_op jit(solution)/shard_map/all_to_all | solution.py:133
  188.3 5.8 %collective-permute-start.13 = (f32[64,768]{1,0:T(8,128)S(1)}, f32[64,768]{1,0:T(8,128)S(1)}, u32[]{:S(2)}, u32[]{:S(2)}) collective-permute-start(f32[64,768]{1,0:T(8,128)S(1)} %broadcast_select_fusion), channel_id=1, source_target_pairs={{0,128},{128,0},{1,129},{129,1},{2,130},{130,2},{3,131},{131,3},{4... | collective-permute-start | bytes 589832 | tf_op jit(solution)/shard_map/ppermute | solution.py:23
  195.1 2.9 %collective-permute-start.14 = (f32[768,384]{1,0:T(8,128)S(1)}, f32[768,384]{1,0:T(8,128)S(1)}, u32[]{:S(2)}, u32[]{:S(2)}) collective-permute-start(f32[768,384]{1,0:T(8,128)S(1)} %dynamic-slice_bitcast_fusion), channel_id=1, source_target_pairs={{0,1},{1,0},{2,3},{3,2},{4,5},{5,4},{6,7},{7,6},{8,9},{9,8},{10,11... | collective-permute-start | bytes 3538952 | tf_op jit(solution)/shard_map/ppermute | solution.py:23
  198.1 34.8 %copy-start.4 = (bf16[8,2,48,384]{3,2,0,1:T(8,128)(2,1)S(1)}, bf16[8,2,48,384]{3,2,0,1:T(8,128)(2,1)}, u32[]{:S(2)}) copy-start(bf16[8,2,48,384]{3,2,0,1:T(8,128)(2,1)} %copy-done.3) | copy-start | bytes 1769476
  198.1 34.8 %copy-start.7 = (bf16[768,384]{1,0:T(8,128)(2,1)S(1)}, bf16[768,384]{1,0:T(8,128)(2,1)}, u32[]{:S(2)}) copy-start(bf16[768,384]{1,0:T(8,128)(2,1)} %copy-done.6) | copy-start | bytes 1769476
  232.8 1.4 collective-permute-start.15
